TPU v7x, 32 devices: a whole 2x2x4 slice. The times are simulated.
32 devices in a mesh: ctx: 4 (over z), head: 8 (over y, x, core).
Axes of the slice: x: 2, y: 2, z: 4, core: 2. Of those that a mesh axis runs over, the one named last changes fastest.
Arguments:
- hyena_query: bfloat16 [2048, 8192], P('ctx', 'head'), may hold values from -6 to 6
- hyena_key: bfloat16 [2048, 8192], P('ctx', 'head'), may hold values from -6 to 6
- hyena_value: bfloat16 [2048, 8192], P('ctx', 'head'), may hold values from -6 to 6
- hyena_filter: bfloat16 [128, 8192], P(None, 'head'), may hold values from -0.5 to 0.5
- attn_query: bfloat16 [2048, 8192], P('ctx', 'head'), may hold values from -100 to 100
- attn_key: bfloat16 [2048, 8192], P('ctx', 'head'), may hold values from -4 to 4
- attn_value: bfloat16 [2048, 8192], P('ctx', 'head'), may hold values from -12 to 12
- segment_ids: int32 [2048], replicated, may hold values from 0 to 5, never falling along the last dimension, each value on 1 to 1024 neighbouring positions
- out_weight: bfloat16 [8192, 8192], P('head'), may hold values from -0.09375 to 0.09375
Outputs:
- hyena_out: bfloat16 [2048, 8192], P('ctx', 'head')
- stream: bfloat16 [2048, 8192], P('ctx', 'head')
Inputs may be any that keep to these rules, and one draw needn't show every extreme that they name: `segment_ids`: never falls along the positions; each document is 1 to 1024 positions in a row, one exactly 1024.
All inputs are finite; a program needn't handle non-finite values.
Results may differ from a plain program's by a relative error of at most 0.014.
Values may be sent and summed in bfloat16 or wider, within the bound.
A program may use at most 320 MiB of HBM per device.

v0:
```python
import functools

import jax
import jax.numpy as jnp
import numpy as np
from jax import lax
from jax.experimental import pallas as pl
from jax.experimental.pallas import tpu as pltpu
from jax.sharding import PartitionSpec as P

HEAD_DIM = 128
LOG2_E = 1.4426950408889634
QUERY_TILE = 256
CHANNEL_TILE = 256


def shifted(x, axis, by):
    devices = lax.axis_size(axis)
    pairs = [(i, i + by) for i in range(devices) if 0 <= i + by < devices]
    return lax.ppermute(x, axis, pairs)


def split_high_low(matrix):
    exact = jnp.asarray(matrix, jnp.float32)
    high = exact.astype(jnp.bfloat16)
    low = (exact - high.astype(jnp.float32)).astype(jnp.bfloat16)
    return high, low


def fourier_matrices(taps):
    size = 2 * taps
    n = np.arange(size)
    k = np.arange(taps)
    angle = 2.0 * np.pi * np.outer(k, n) / size
    alternating = np.where(n % 2 == 0, 1.0, -1.0)
    forward = np.concatenate([np.cos(angle), alternating[None], np.sin(angle)[1:]], axis=0)
    gain = np.full((size,), 2.0 / size)
    gain[0] = gain[taps] = 1.0 / size
    inverse = (forward * gain[:, None]).T[taps:]
    return forward.astype(np.float32), inverse.astype(np.float32)


def dot32(a, b):
    return jnp.dot(a, b, preferred_element_type=jnp.float32)


def hyena_kernel(rim_ref, query_ref, key_ref, value_ref, taps_ref, fh_ref, fl_ref, gh_ref, gl_ref, out_ref):
    rows, _ = key_ref.shape
    taps = taps_ref.shape[0]
    fh, fl, gh, gl = fh_ref[...], fl_ref[...], gh_ref[...], gl_ref[...]
    tap_freq = dot32(fh[:, :taps], taps_ref[...]) + dot32(fl[:, :taps], taps_ref[...])
    tap_cos, tap_sin = tap_freq[:taps], tap_freq[taps:]
    edge = lax.broadcasted_iota(jnp.int32, tap_cos.shape, 0) == 0
    before = rim_ref[...]
    for block in range(rows // taps):
        here = slice(block * taps, (block + 1) * taps)
        now = (key_ref[here, :].astype(jnp.float32) * value_ref[here, :].astype(jnp.float32)).astype(jnp.bfloat16)
        window = jnp.concatenate([before, now], axis=0)
        freq = dot32(fh, window) + dot32(fl, window)
        cos, sin = freq[:taps], freq[taps:]
        sin_sin = sin * tap_sin
        real = cos * tap_cos - jnp.where(edge, 0.0, sin_sin)
        imag = jnp.where(edge, sin_sin, cos * tap_sin + sin * tap_cos)
        product = jnp.concatenate([real, imag], axis=0)
        high = product.astype(jnp.bfloat16)
        low = (product - high.astype(jnp.float32)).astype(jnp.bfloat16)
        filtered = dot32(gh, high) + dot32(gh, low) + dot32(gl, high)
        out_ref[here, :] = (query_ref[here, :].astype(jnp.float32) * filtered).astype(jnp.bfloat16)
        before = now


def hyena(rim, query, key, value, taps):
    rows, width = key.shape
    tap_count = taps.shape[0]
    forward, inverse = fourier_matrices(tap_count)
    constants = split_high_low(forward) + split_high_low(inverse)
    column = lambda r: pl.BlockSpec((r, CHANNEL_TILE), lambda i: (0, i))
    whole = lambda a: pl.BlockSpec(a.shape, lambda i: (0, 0))
    return pl.pallas_call(
        hyena_kernel,
        out_shape=jax.ShapeDtypeStruct((rows, width), jnp.bfloat16),
        grid=(width // CHANNEL_TILE,),
        in_specs=[column(tap_count), column(rows), column(rows), column(rows), column(tap_count)]
        + [whole(a) for a in constants],
        out_specs=column(rows),
        compiler_params=pltpu.CompilerParams(vmem_limit_bytes=48 * 2**20),
        cost_estimate=pl.CostEstimate(flops=3 * 10**9, bytes_accessed=5 * 2**20, transcendentals=0),
    )(rim, query, key, value, taps, *constants)


def attention_kernel(hops, start_ref, query_ref, *refs):
    key_refs, value_refs, out_ref = refs[: hops + 1], refs[hops + 1 : 2 * hops + 2], refs[-1]
    rows = query_ref.shape[0]
    scale = HEAD_DIM ** (-0.5) * LOG2_E
    for tile in range(rows // QUERY_TILE):
        low, high = tile * QUERY_TILE, (tile + 1) * QUERY_TILE
        query = query_ref[low:high, :]
        start = start_ref[low:high, :]
        parts = []
        for back in range(hops, -1, -1):
            first = low if back == hops else 0
            last = high if back == 0 else rows
            scores = lax.dot_general(
                query, key_refs[back][first:last, :], (((1,), (1,)), ((), ())), preferred_element_type=jnp.float32
            )
            position = lax.broadcasted_iota(jnp.int32, scores.shape, 1) + (first - back * rows)
            allowed = position >= start
            if back == 0:
                allowed &= position <= lax.broadcasted_iota(jnp.int32, scores.shape, 0) + low
            parts.append((back, first, last, jnp.where(allowed, scores, -1e30)))
        top = functools.reduce(jnp.maximum, [jnp.max(part[3], axis=1, keepdims=True) for part in parts])
        total = jnp.zeros((QUERY_TILE, 1), jnp.float32)
        weighted = jnp.zeros((QUERY_TILE, HEAD_DIM), jnp.float32)
        for back, first, last, scores in parts:
            probs = jnp.exp2((scores - top) * scale)
            total += jnp.sum(probs, axis=1, keepdims=True)
            weighted += dot32(probs.astype(jnp.bfloat16), value_refs[back][first:last, :])
        out_ref[low:high, :] = (weighted / total).astype(jnp.bfloat16)


def attention(start, query, keys, values):
    rows, width = query.shape
    hops = len(keys) - 1
    head = pl.BlockSpec((rows, HEAD_DIM), lambda h: (0, h))
    return pl.pallas_call(
        functools.partial(attention_kernel, hops),
        out_shape=jax.ShapeDtypeStruct((rows, width), jnp.bfloat16),
        grid=(width // HEAD_DIM,),
        in_specs=[pl.BlockSpec((rows, 1), lambda h: (0, 0)), head] + [head] * (2 * hops + 2),
        out_specs=head,
        compiler_params=pltpu.CompilerParams(vmem_limit_bytes=48 * 2**20),
        cost_estimate=pl.CostEstimate(flops=4 * 10**9, bytes_accessed=8 * 2**20, transcendentals=6 * 10**6),
    )(start, query, *keys, *values)


def on_device(
    hyena_query,
    hyena_key,
    hyena_value,
    hyena_filter,
    attn_query,
    attn_key,
    attn_value,
    segment_ids,
    out_weight,
):
    num_rows = hyena_key.shape[0]
    tap_count = hyena_filter.shape[0]
    hops = lax.axis_size("ctx") // 2
    last_key = hyena_key[num_rows - tap_count :].astype(jnp.float32)
    last_value = hyena_value[num_rows - tap_count :].astype(jnp.float32)
    rim = shifted((last_key * last_value).astype(jnp.bfloat16), "ctx", 1)
    keys, values = [attn_key], [attn_value]
    for _ in range(hops):
        keys.append(shifted(keys[-1], "ctx", 1))
        values.append(shifted(values[-1], "ctx", 1))
    hyena_out = hyena(rim, hyena_query, hyena_key, hyena_value, hyena_filter)
    offset = lax.axis_index("ctx") * num_rows
    own_segments = lax.dynamic_slice_in_dim(segment_ids, offset, num_rows)
    document_start = jnp.sum((segment_ids[None, :] < own_segments[:, None]).astype(jnp.int32), axis=1)
    start = (document_start - offset)[:, None]
    attended = attention(start, attn_query, keys, values)
    partial_terms = jnp.dot(attended, out_weight, preferred_element_type=jnp.float32)
    projected = lax.psum_scatter(
        partial_terms.astype(jnp.bfloat16), "head", scatter_dimension=1, tiled=True
    ).astype(jnp.float32)
    stream = (hyena_out.astype(jnp.float32) + projected).astype(jnp.bfloat16)
    return (hyena_out, stream)


def solution(mesh):
    return jax.shard_map(
        on_device,
        mesh=mesh,
        in_specs=(
            P("ctx", "head"),
            P("ctx", "head"),
            P("ctx", "head"),
            P(None, "head"),
            P("ctx", "head"),
            P("ctx", "head"),
            P("ctx", "head"),
            P(),
            P("head", None),
        ),
        out_specs=(P("ctx", "head"), P("ctx", "head")),
        check_vma=False,
    )
```

profile of v0, /device:TPU:16, one launch (start us, length us, event | category | flops | bytes accessed | tf_op | source)
XLA Modules:
  0.0 216.7 jit_solution(4842378460505812442)
XLA Ops:
  7.2 0.0 reduce-scatter.2.cloned.1.call-start
  7.2 3.5 %collective-permute-start.1 = (bf16[512,1024]{1,0:T(8,128)(2,1)}, bf16[512,1024]{1,0:T(8,128)(2,1)S(1)}, u32[]{:S(2)}, u32[]{:S(2)}) collective-permute-start(bf16[512,1024]{1,0:T(8,128)(2,1)} %refs_0_.1), channel_id=1, source_target_pairs={{0,8},{8,16},{16,24},{1,9},{9,17},{17,25},{2,10},{10,18},{18,26},{... | collective-permute-start | bytes 3145736 | tf_op jit(solution)/shard_map/ppermute | solution.py:20
  10.7 1.9 collective-permute-start.3
  12.6 22.7 %collective-permute-done.1.refs_1_ = bf16[512,1024]{1,0:T(8,128)(2,1)S(1)} collective-permute-done((bf16[512,1024]{1,0:T(8,128)(2,1)}, bf16[512,1024]{1,0:T(8,128)(2,1)S(1)}, u32[]{:S(2)}, u32[]{:S(2)}) %collective-permute-start.1) | collective-permute-done | bytes 1048608 | tf_op jit(solution)/shard_map/ppermute | solution.py:20
  35.4 3.5 %collective-permute-start.2 = (bf16[512,1024]{1,0:T(8,128)(2,1)S(1)}, bf16[512,1024]{1,0:T(8,128)(2,1)S(1)}, u32[]{:S(2)}, u32[]{:S(2)}) collective-permute-start(bf16[512,1024]{1,0:T(8,128)(2,1)S(1)} %collective-permute-done.1.refs_1_), channel_id=1, source_target_pairs={{0,8},{8,16},{16,24},{1,9},{9,17},{17,25},{2,10},{10,18},{18,26},{... | collective-permute-start | bytes 3145736 | tf_op jit(solution)/shard_map/ppermute | solution.py:20
  38.8 19.0 %collective-permute-done.3.refs_4_ = bf16[512,1024]{1,0:T(8,128)(2,1)S(1)} collective-permute-done((bf16[512,1024]{1,0:T(8,128)(2,1)}, bf16[512,1024]{1,0:T(8,128)(2,1)S(1)}, u32[]{:S(2)}, u32[]{:S(2)}) %collective-permute-start.3) | collective-permute-done | bytes 1048608 | tf_op jit(solution)/shard_map/ppermute | solution.py:20
  57.8 0.0 copy-start.10
  57.8 3.5 %collective-permute-start.4 = (bf16[512,1024]{1,0:T(8,128)(2,1)S(1)}, bf16[512,1024]{1,0:T(8,128)(2,1)}, u32[]{:S(2)}, u32[]{:S(2)}) collective-permute-start(bf16[512,1024]{1,0:T(8,128)(2,1)S(1)} %collective-permute-done.3.refs_4_), channel_id=1, source_target_pairs={{0,8},{8,16},{16,24},{1,9},{9,17},{17,25},{2,10},{10,18},{18,26},{... | collective-permute-start | bytes 3145736 | tf_op jit(solution)/shard_map/ppermute | solution.py:20
  61.3 0.8 dynamic_slice.3
  62.1 1.3 convert_reduce_fusion
  63.3 0.2 copy.14.start_ref
  63.5 16.8 %collective-permute-done.2.refs_2_ = bf16[512,1024]{1,0:T(8,128)(2,1)S(1)} collective-permute-done((bf16[512,1024]{1,0:T(8,128)(2,1)S(1)}, bf16[512,1024]{1,0:T(8,128)(2,1)S(1)}, u32[]{:S(2)}, u32[]{:S(2)}) %collective-permute-start.2) | collective-permute-done | bytes 1048608 | tf_op jit(solution)/shard_map/ppermute | solution.py:20
  80.3 21.4 %collective-permute-done.4.refs_5_ = bf16[512,1024]{1,0:T(8,128)(2,1)} collective-permute-done((bf16[512,1024]{1,0:T(8,128)(2,1)S(1)}, bf16[512,1024]{1,0:T(8,128)(2,1)}, u32[]{:S(2)}, u32[]{:S(2)}) %collective-permute-start.4) | collective-permute-done | bytes 1048608 | tf_op jit(solution)/shard_map/ppermute | solution.py:20
  101.7 0.0 copy-done.10
  101.7 0.0 copy-start.2
  101.7 1.2 copy-done.2
  103.0 0.0 copy-start.3
  103.0 1.2 copy-done.3
  104.2 13.4 %shard_map.123 = bf16[512,1024]{1,0:T(8,128)(2,1)S(1)} custom-call(s32[512,1]{1,0:T(8,128)S(1)} %copy.14.start_ref, bf16[512,1024]{1,0:T(8,128)(2,1)S(1)} %copy-done.2, bf16[512,1024]{1,0:T(8,128)(2,1)S(1)} %copy-done.3, bf16[512,1024]{1,0:T(8,128)(2,1)S(1)} %collective-permute-done.1.refs_1_, bf16[512,1024]{1,0:T(8,128)(2,1)S(1)} %collective-permute-done.2.refs_2_, ...), custom_call_target="tpu_custom_call" | custom-call | flops 4000000000 | bytes 8388608 | tf_op jit(solution)/shard_map/pallas_call | solution.py:125
  117.6 16.8 %convolution_convert_fusion = bf16[512,8192]{1,0:T(8,128)(2,1)} fusion(bf16[512,1024]{1,0:T(8,128)(2,1)S(1)} %shard_map.123, bf16[1024,8192]{1,0:T(8,128)(2,1)} %param.19), kind=kOutput, calls=%fused_computation | convolution fusion | flops 8594128896 | bytes 26214400 | tf_op jit(solution)/shard_map/dot_general | solution.py:163
  134.4 0.0 copy-start
  134.4 0.0 copy-start.1
  134.4 0.0 copy-start.4
  134.4 0.0 copy-start.5
  134.4 0.0 copy-start.6
  134.4 0.0 reduce-scatter.2.cloned.1.call-update
  134.4 1.2 copy-done
  135.6 0.3 copy-done.1
  135.9 0.1 multiply_convert_fusion
  136.0 3.5 %collective-permute-start = (bf16[128,1024]{1,0:T(8,128)(2,1)S(1)}, bf16[128,1024]{1,0:T(8,128)(2,1)S(1)}, u32[]{:S(2)}, u32[]{:S(2)}) collective-permute-start(bf16[128,1024]{1,0:T(8,128)(2,1)S(1)} %multiply_convert_fusion), channel_id=1, source_target_pairs={{0,8},{8,16},{16,24},{1,9},{9,17},{17,25},{2,10},{10,18},{18,26},{... | collective-permute-start | bytes 786440 | tf_op jit(solution)/shard_map/ppermute | solution.py:20
  139.5 5.6 %collective-permute-done.rim_ref = bf16[128,1024]{1,0:T(8,128)(2,1)S(1)} collective-permute-done((bf16[128,1024]{1,0:T(8,128)(2,1)S(1)}, bf16[128,1024]{1,0:T(8,128)(2,1)S(1)}, u32[]{:S(2)}, u32[]{:S(2)}) %collective-permute-start) | collective-permute-done | bytes 262176 | tf_op jit(solution)/shard_map/ppermute | solution.py:20
  145.0 0.0 copy-done.4
  145.0 0.0 copy-done.5
  145.1 0.0 copy-done.6
  145.1 0.0 copy-start.7
  145.1 0.9 copy-done.7
  146.0 0.0 copy-start.8
  146.0 0.8 copy-done.8
  146.8 0.0 copy-start.9
  146.8 0.8 copy-done.9
  147.7 5.1 %shard_map.122 = bf16[512,1024]{1,0:T(8,128)(2,1)} custom-call(bf16[128,1024]{1,0:T(8,128)(2,1)S(1)} %collective-permute-done.rim_ref, bf16[512,1024]{1,0:T(8,128)(2,1)S(1)} %copy-done.4, bf16[512,1024]{1,0:T(8,128)(2,1)S(1)} %copy-done.1, bf16[512,1024]{1,0:T(8,128)(2,1)S(1)} %copy-done, bf16[128,1024]{1,0:T(8,128)(2,1)S(1)} %copy-done.5, ...), custom_call_target="tpu_custom_call" | custom-call | flops 3000000000 | bytes 5242880 | tf_op jit(solution)/shard_map/pallas_call | solution.py:79
  152.8 54.1 %reduce-scatter.2.cloned.1.call-done = bf16[512,1024]{1,0:T(8,128)(2,1)} async-done(((bf16[512,8192]{1,0:T(8,128)(2,1)}), bf16[512,1024]{1,0:T(8,128)(2,1)}) %reduce-scatter.2.cloned.1.call-update) | async-done | bytes 1048592 | tf_op jit(solution)/shard_map/reduce_scatter | solution.py:164
  206.9 2.9 %add_convert_fusion = bf16[512,1024]{1,0:T(8,128)(2,1)} fusion(bf16[512,1024]{1,0:T(8,128)(2,1)} %reduce-scatter.2.cloned.1.call-done, bf16[512,1024]{1,0:T(8,128)(2,1)} %shard_map.122), kind=kLoop, calls=%fused_computation.2 | loop fusion | flops 2097152 | bytes 3145728 | tf_op jit(solution)/shard_map/convert_element_type | solution.py:167
  (1 shorter events, 0.0 us)
Async XLA Ops:
  7.2 199.8 %reduce-scatter.2.cloned.1.call-start = ((), (), s32[]{:S(2)}) async-start(), calls=%async_computation.1 | async-start | bytes 9437184 | tf_op jit(solution)/shard_map/reduce_scatter | solution.py:164
  7.2 28.2 %collective-permute-start.1 = (bf16[512,1024]{1,0:T(8,128)(2,1)}, bf16[512,1024]{1,0:T(8,128)(2,1)S(1)}, u32[]{:S(2)}, u32[]{:S(2)}) collective-permute-start(bf16[512,1024]{1,0:T(8,128)(2,1)} %refs_0_.1), channel_id=1, source_target_pairs={{0,8},{8,16},{16,24},{1,9},{9,17},{17,25},{2,10},{10,18},{18,26},{... | collective-permute-start | bytes 3145736 | tf_op jit(solution)/shard_map/ppermute | solution.py:20
  10.7 47.1 %collective-permute-start.3 = (bf16[512,1024]{1,0:T(8,128)(2,1)}, bf16[512,1024]{1,0:T(8,128)(2,1)S(1)}, u32[]{:S(2)}, u32[]{:S(2)}) collective-permute-start(bf16[512,1024]{1,0:T(8,128)(2,1)} %refs_3_.1), channel_id=1, source_target_pairs={{0,8},{8,16},{16,24},{1,9},{9,17},{17,25},{2,10},{10,18},{18,26},{... | collective-permute-start | bytes 3145736 | tf_op jit(solution)/shard_map/ppermute | solution.py:20
  35.4 44.9 %collective-permute-start.2 = (bf16[512,1024]{1,0:T(8,128)(2,1)S(1)}, bf16[512,1024]{1,0:T(8,128)(2,1)S(1)}, u32[]{:S(2)}, u32[]{:S(2)}) collective-permute-start(bf16[512,1024]{1,0:T(8,128)(2,1)S(1)} %collective-permute-done.1.refs_1_), channel_id=1, source_target_pairs={{0,8},{8,16},{16,24},{1,9},{9,17},{17,25},{2,10},{10,18},{18,26},{... | collective-permute-start | bytes 3145736 | tf_op jit(solution)/shard_map/ppermute | solution.py:20
  57.8 43.9 %copy-start.10 = (bf16[512,1024]{1,0:T(8,128)(2,1)}, bf16[512,1024]{1,0:T(8,128)(2,1)S(1)}, u32[]{:S(2)}) copy-start(bf16[512,1024]{1,0:T(8,128)(2,1)S(1)} %collective-permute-done.3.refs_4_) | copy-start | bytes 3145732
  57.8 43.9 %collective-permute-start.4 = (bf16[512,1024]{1,0:T(8,128)(2,1)S(1)}, bf16[512,1024]{1,0:T(8,128)(2,1)}, u32[]{:S(2)}, u32[]{:S(2)}) collective-permute-start(bf16[512,1024]{1,0:T(8,128)(2,1)S(1)} %collective-permute-done.3.refs_4_), channel_id=1, source_target_pairs={{0,8},{8,16},{16,24},{1,9},{9,17},{17,25},{2,10},{10,18},{18,26},{... | collective-permute-start | bytes 3145736 | tf_op jit(solution)/shard_map/ppermute | solution.py:20
  101.7 1.2 copy-start.2
  103.0 1.2 copy-start.3
  134.4 1.2 copy-start
  134.4 1.5 copy-start.1
  134.4 10.7 %copy-start.4 = (bf16[512,1024]{1,0:T(8,128)(2,1)S(1)}, bf16[512,1024]{1,0:T(8,128)(2,1)}, u32[]{:S(2)}) copy-start(bf16[512,1024]{1,0:T(8,128)(2,1)} %query_ref.2) | copy-start | bytes 3145732
  134.4 10.7 %copy-start.5 = (bf16[128,1024]{1,0:T(8,128)(2,1)S(1)}, bf16[128,1024]{1,0:T(8,128)(2,1)}, u32[]{:S(2)}) copy-start(bf16[128,1024]{1,0:T(8,128)(2,1)} %taps_ref.1) | copy-start | bytes 786436
  134.4 10.7 %copy-start.6 = (bf16[256,256]{1,0:T(8,128)(2,1)S(1)}, bf16[256,256]{1,0:T(8,128)(2,1)}, u32[]{:S(2)}) copy-start(bf16[256,256]{1,0:T(8,128)(2,1)} %constant.17.fh_ref) | copy-start | bytes 393220
  136.0 9.1 %collective-permute-start = (bf16[128,1024]{1,0:T(8,128)(2,1)S(1)}, bf16[128,1024]{1,0:T(8,128)(2,1)S(1)}, u32[]{:S(2)}, u32[]{:S(2)}) collective-permute-start(bf16[128,1024]{1,0:T(8,128)(2,1)S(1)} %multiply_convert_fusion), channel_id=1, source_target_pairs={{0,8},{8,16},{16,24},{1,9},{9,17},{17,25},{2,10},{10,18},{18,26},{... | collective-permute-start | bytes 786440 | tf_op jit(solution)/shard_map/ppermute | solution.py:20
  145.1 0.9 copy-start.7
  146.0 0.8 copy-start.8
  146.8 0.8 copy-start.9
Sparse Core Ops, SparseCore 0:
  134.5 72.3 reduce-scatter.1
where the time goes:
time: 219 us; the launch traced here: 217 us
  waiting for transfers between devices  140 us (64%)
  Pallas kernels  18.5 us (8%)
  matrix products  16.8 us (8%)
  starting transfers between devices  15.9 us (7%)
  between operations  14.1 us (6%)
  local copies, waits for them, and re-layouts  7.5 us (3%)
  other arithmetic  4.23 us (2%)
    ppermute x5, waiting for transfers between devices, shifted(): return lax.ppermute(x, axis, pairs)  85.5 us
    reduce_scatter x1, waiting for transfers between devices, on_device(): lax.psum_scatter(partial_terms.astype(jnp.bfloat16), 'head', scatter_dime...  54.1 us
    dot_general x1, matrix products, on_device(): jnp.dot(attended, out_weight, preferred_element_type=jnp.float32)  16.8 us
    ppermute x5, starting transfers between devices, shifted(): return lax.ppermute(x, axis, pairs)  15.8 us
    pallas_call x1, Pallas kernels, attention(): pl.pallas_call(functools.partial(attention_kernel, hops), out_shape=jax.S...  13.4 us
    unnamed x22, local copies, waits for them, and re-layouts  6.59 us
    pallas_call x1, Pallas kernels, hyena(): pl.pallas_call(hyena_kernel, out_shape=jax.ShapeDtypeStruct((rows, width)...  5.1 us
  transfers between devices with their start and end apart: 6, of which 6 were waited for; matrix products, arithmetic and copies ran while one was open for 1% of the time, Pallas kernels for 2%

commit v1 on v0

--- a/solution.py
+++ b/solution.py
@@ -12,6 +12,8 @@
 LOG2_E = 1.4426950408889634
 QUERY_TILE = 256
 CHANNEL_TILE = 256
+PROJECT_ROWS = 128
+MESH = pl.DeviceIdType.MESH
 
 
 def shifted(x, axis, by):
@@ -133,6 +135,150 @@
     )(start, query, *keys, *values)
 
 
+def project_kernel(n, chunk, attended_ref, hyena_ref, weight_ref, out_ref, weights, away, near, landed, load_sem, send_sem, recv_sem):
+    rows, width = out_ref.shape
+    chunks = rows // chunk
+    stages = n.bit_length() - 1
+    me = lax.axis_index("head")
+    core = me % 2
+
+    def flip(bit, by):
+        return bit + by - 2 * bit * by
+
+    def slot_bit(slot, stage):
+        return (slot // (n >> (stage + 1))) % 2
+
+    def destination(slot):
+        to_core = flip(core, slot_bit(slot, 0))
+        place = to_core
+        for axis in range(1, stages):
+            across = slot_bit(slot, axis) * (1 - to_core) + slot_bit(slot, stages - axis) * to_core
+            place = place + flip((me // 2**axis) % 2, across) * 2**axis
+        return place
+
+    def partner(stage):
+        if stage == 0:
+            return me + 1 - 2 * core
+        forward = me + (1 - 2 * ((me // 2**stage) % 2)) * 2**stage
+        other = stages - stage
+        backward = me + (1 - 2 * ((me // 2**other) % 2)) * 2**other
+        return forward * (1 - core) + backward * core
+
+    loads = []
+    for slot in list(range(n // 2, n)) + list(range(n // 2)):
+        columns = pl.ds(pl.multiple_of(destination(slot) * width, width), width)
+        load = pltpu.make_async_copy(weight_ref.at[:, columns], weights.at[slot], load_sem.at[slot])
+        load.start()
+        loads.append((slot, load))
+
+    barrier = pltpu.get_barrier_semaphore()
+    for stage in range(stages):
+        pl.semaphore_signal(barrier, inc=1, device_id={"head": partner(stage)}, device_id_type=MESH)
+    pl.semaphore_wait(barrier, stages)
+
+    first_of = [n - (n >> stage) for stage in range(stages)]
+
+    def copy(stage, part):
+        count = n >> (stage + 1)
+        source = away.at[part] if stage == 0 else near.at[part, pl.ds(count, count)]
+        return pltpu.make_async_remote_copy(
+            src_ref=source,
+            dst_ref=landed.at[part, pl.ds(first_of[stage], count)],
+            send_sem=send_sem.at[stage, part],
+            recv_sem=recv_sem.at[stage, part],
+            device_id={"head": partner(stage)},
+            device_id_type=MESH,
+        )
+
+    def term(part, slot):
+        return jnp.dot(
+            attended_ref[part * chunk : (part + 1) * chunk, :], weights[slot], preferred_element_type=jnp.float32
+        )
+
+    def far_terms(part):
+        if part == 0:
+            for _, load in loads[: n // 2]:
+                load.wait()
+
+        @pl.loop(0, n // 2)
+        def _(index):
+            away[part, index] = term(part, index + n // 2).astype(jnp.bfloat16)
+
+        copy(0, part).start()
+
+    def near_terms(part):
+        if part == 0:
+            for _, load in loads[n // 2 :]:
+                load.wait()
+        copy(0, part).wait_recv()
+
+        def add(index):
+            total = term(part, index) + landed[part, index].astype(jnp.float32)
+            near[part, index] = total.astype(jnp.bfloat16)
+
+        pl.loop(n // 4, n // 2)(add)
+        copy(1, part).start()
+        pl.loop(0, n // 4)(add)
+
+    def fold(stage, part):
+        copy(stage, part).wait_recv()
+        half = n >> (stage + 2)
+
+        def add(index):
+            arrived = landed[part, first_of[stage] + index].astype(jnp.float32)
+            near[part, index] = (near[part, index].astype(jnp.float32) + arrived).astype(jnp.bfloat16)
+
+        pl.loop(half, 2 * half)(add)
+        copy(stage + 1, part).start()
+        pl.loop(0, half)(add)
+
+    def finish(part):
+        last = stages - 1
+        copy(last, part).wait_recv()
+        here = slice(part * chunk, (part + 1) * chunk)
+        total = near[part, 0].astype(jnp.float32) + landed[part, first_of[last]].astype(jnp.float32)
+        out_ref[here, :] = (hyena_ref[here, :].astype(jnp.float32) + total).astype(jnp.bfloat16)
+
+    for step in range(chunks + stages):
+        if step < chunks:
+            far_terms(step)
+        for stage in range(1, stages):
+            if 0 <= step - stage < chunks:
+                near_terms(step - 1) if stage == 1 else fold(stage - 1, step - stage)
+        if 0 <= step - stages < chunks:
+            finish(step - stages)
+    for stage in range(stages):
+        for part in range(chunks):
+            copy(stage, part).wait_send()
+
+
+def project(attended, hyena_out, weight):
+    rows, width = attended.shape
+    n = lax.axis_size("head")
+    chunks = rows // PROJECT_ROWS
+    stages = n.bit_length() - 1
+    vmem = pl.BlockSpec(memory_space=pltpu.VMEM)
+    return pl.pallas_call(
+        functools.partial(project_kernel, n, PROJECT_ROWS),
+        out_shape=jax.ShapeDtypeStruct((rows, width), jnp.bfloat16),
+        in_specs=[vmem, vmem, pl.BlockSpec(memory_space=pl.ANY)],
+        out_specs=vmem,
+        scratch_shapes=[
+            pltpu.VMEM((n, width, width), jnp.bfloat16),
+            pltpu.VMEM((chunks, n // 2, PROJECT_ROWS, width), jnp.bfloat16),
+            pltpu.VMEM((chunks, n // 2, PROJECT_ROWS, width), jnp.bfloat16),
+            pltpu.VMEM((chunks, n - 1, PROJECT_ROWS, width), jnp.bfloat16),
+            pltpu.SemaphoreType.DMA((n,)),
+            pltpu.SemaphoreType.DMA((stages, chunks)),
+            pltpu.SemaphoreType.DMA((stages, chunks)),
+        ],
+        compiler_params=pltpu.CompilerParams(
+            collective_id=0, has_side_effects=True, vmem_limit_bytes=56 * 2**20
+        ),
+        cost_estimate=pl.CostEstimate(flops=9 * 10**9, bytes_accessed=20 * 2**20, transcendentals=0),
+    )(attended, hyena_out, weight)
+
+
 def on_device(
     hyena_query,
     hyena_key,
@@ -159,12 +305,9 @@
     own_segments = lax.dynamic_slice_in_dim(segment_ids, offset, num_rows)
     document_start = jnp.sum((segment_ids[None, :] < own_segments[:, None]).astype(jnp.int32), axis=1)
     start = (document_start - offset)[:, None]
+    start, hyena_out = lax.optimization_barrier((start, hyena_out))
     attended = attention(start, attn_query, keys, values)
-    partial_terms = jnp.dot(attended, out_weight, preferred_element_type=jnp.float32)
-    projected = lax.psum_scatter(
-        partial_terms.astype(jnp.bfloat16), "head", scatter_dimension=1, tiled=True
-    ).astype(jnp.float32)
-    stream = (hyena_out.astype(jnp.float32) + projected).astype(jnp.bfloat16)
+    stream = project(attended, hyena_out, out_weight)
     return (hyena_out, stream)
 
 

time: 219 us -> 183 us (0.84)
  waiting for transfers between devices: 140 us -> 82.6 us
  Pallas kernels: 18.5 us -> 69.1 us
  matrix products: 16.8 us -> 0 us
  between operations: 14.1 us -> 0.75 us
  local copies, waits for them, and re-layouts: 7.5 us -> 12.3 us
    reduce_scatter x1 -> x0, waiting for transfers between devices: 54.1 us -> none  [on_device(): lax.psum_scatter(partial_terms.astype(jnp.bfloat16), 'head', scatter_dime...]
    pallas_call x0 -> x1, Pallas kernels: none -> 50.8 us  [project(): pl.pallas_call(functools.partial(project_kernel, n, PROJECT_ROWS), out_sh...]
    dot_general x1 -> x0, matrix products: 16.8 us -> none  [on_device(): jnp.dot(attended, out_weight, preferred_element_type=jnp.float32)]
    unnamed x22 -> x23, local copies, waits for them, and re-layouts: 6.59 us -> 11.3 us
    ppermute x5, waiting for transfers between devices: 85.5 us -> 82.6 us  [shifted(): return lax.ppermute(x, axis, pairs)]
    convert_element_type x1 -> x0, other arithmetic: 2.91 us -> none  [on_device(): stream = (hyena_out.astype(jnp.float32) + projected).astype(jnp.bfloat16)]
  transfers between devices with their start and end apart: 6 -> 5, of which waited for: 6 -> 3; matrix products, arithmetic and copies ran while one was open for 1% -> 2% of each run, Pallas kernels for 2% -> 3%
where the time goes in v1:
time: 183 us; the launch traced here: 181 us
  waiting for transfers between devices  82.6 us (45%)
  Pallas kernels  69.1 us (38%)
  starting transfers between devices  14.3 us (8%)
  local copies, waits for them, and re-layouts  12.3 us (7%)
  other arithmetic  2.36 us (1%)
    ppermute x5, waiting for transfers between devices, shifted(): return lax.ppermute(x, axis, pairs)  82.6 us
    pallas_call x1, Pallas kernels, project(): pl.pallas_call(functools.partial(project_kernel, n, PROJECT_ROWS), out_sh...  50.8 us
    ppermute x5, starting transfers between devices, shifted(): return lax.ppermute(x, axis, pairs)  14.3 us
    pallas_call x1, Pallas kernels, attention(): pl.pallas_call(functools.partial(attention_kernel, hops), out_shape=jax.S...  13.2 us
    unnamed x23, local copies, waits for them, and re-layouts  11.3 us
    pallas_call x1, Pallas kernels, hyena(): pl.pallas_call(hyena_kernel, out_shape=jax.ShapeDtypeStruct((rows, width)...  5.11 us
  transfers between devices with their start and end apart: 5, of which 3 were waited for; matrix products, arithmetic and copies ran while one was open for 2% of the time, Pallas kernels for 3%

profile of v1, /device:TPU:16, one launch (start us, length us, event | category | flops | bytes accessed | tf_op | source)
XLA Modules:
  0.0 181.4 jit_solution(14823740917927000600)
XLA Ops:
  0.6 3.5 %collective-permute-start.1 = (bf16[512,1024]{1,0:T(8,128)(2,1)}, bf16[512,1024]{1,0:T(8,128)(2,1)S(1)}, u32[]{:S(2)}, u32[]{:S(2)}) collective-permute-start(bf16[512,1024]{1,0:T(8,128)(2,1)} %refs_0_.1), channel_id=1, source_target_pairs={{0,8},{8,16},{16,24},{1,9},{9,17},{17,25},{2,10},{10,18},{18,26},{... | collective-permute-start | bytes 3145736 | tf_op jit(solution)/shard_map/ppermute | solution.py:22
  4.1 1.9 %collective-permute-start.3 = (bf16[512,1024]{1,0:T(8,128)(2,1)}, bf16[512,1024]{1,0:T(8,128)(2,1)}, u32[]{:S(2)}, u32[]{:S(2)}) collective-permute-start(bf16[512,1024]{1,0:T(8,128)(2,1)} %refs_3_.1), channel_id=1, source_target_pairs={{0,8},{8,16},{16,24},{1,9},{9,17},{17,25},{2,10},{10,18},{18,26},{... | collective-permute-start | bytes 3145736 | tf_op jit(solution)/shard_map/ppermute | solution.py:22
  6.1 22.7 %collective-permute-done.1.refs_1_ = bf16[512,1024]{1,0:T(8,128)(2,1)S(1)} collective-permute-done((bf16[512,1024]{1,0:T(8,128)(2,1)}, bf16[512,1024]{1,0:T(8,128)(2,1)S(1)}, u32[]{:S(2)}, u32[]{:S(2)}) %collective-permute-start.1) | collective-permute-done | bytes 1048608 | tf_op jit(solution)/shard_map/ppermute | solution.py:22
  28.8 3.5 %collective-permute-start.2 = (bf16[512,1024]{1,0:T(8,128)(2,1)S(1)}, bf16[512,1024]{1,0:T(8,128)(2,1)}, u32[]{:S(2)}, u32[]{:S(2)}) collective-permute-start(bf16[512,1024]{1,0:T(8,128)(2,1)S(1)} %collective-permute-done.1.refs_1_), channel_id=1, source_target_pairs={{0,8},{8,16},{16,24},{1,9},{9,17},{17,25},{2,10},{10,18},{18,26},{... | collective-permute-start | bytes 3145736 | tf_op jit(solution)/shard_map/ppermute | solution.py:22
  32.3 19.1 %collective-permute-done.3.refs_4_ = bf16[512,1024]{1,0:T(8,128)(2,1)} collective-permute-done((bf16[512,1024]{1,0:T(8,128)(2,1)}, bf16[512,1024]{1,0:T(8,128)(2,1)}, u32[]{:S(2)}, u32[]{:S(2)}) %collective-permute-start.3) | collective-permute-done | bytes 1048608 | tf_op jit(solution)/shard_map/ppermute | solution.py:22
  51.4 3.5 %collective-permute-start.4 = (bf16[512,1024]{1,0:T(8,128)(2,1)}, bf16[512,1024]{1,0:T(8,128)(2,1)}, u32[]{:S(2)}, u32[]{:S(2)}) collective-permute-start(bf16[512,1024]{1,0:T(8,128)(2,1)} %collective-permute-done.3.refs_4_), channel_id=1, source_target_pairs={{0,8},{8,16},{16,24},{1,9},{9,17},{17,25},{2,10},{10,18},{18,26},{... | collective-permute-start | bytes 3145736 | tf_op jit(solution)/shard_map/ppermute | solution.py:22
  54.8 1.1 multiply_convert_fusion
  55.9 1.9 %collective-permute-start = (bf16[128,1024]{1,0:T(8,128)(2,1)S(1)}, bf16[128,1024]{1,0:T(8,128)(2,1)S(1)}, u32[]{:S(2)}, u32[]{:S(2)}) collective-permute-start(bf16[128,1024]{1,0:T(8,128)(2,1)S(1)} %multiply_convert_fusion), channel_id=1, source_target_pairs={{0,8},{8,16},{16,24},{1,9},{9,17},{17,25},{2,10},{10,18},{18,26},{... | collective-permute-start | bytes 786440 | tf_op jit(solution)/shard_map/ppermute | solution.py:22
  57.9 0.8 dynamic_slice.3
  58.6 1.3 convert_reduce_fusion
  59.9 40.8 %collective-permute-done.rim_ref = bf16[128,1024]{1,0:T(8,128)(2,1)S(1)} collective-permute-done((bf16[128,1024]{1,0:T(8,128)(2,1)S(1)}, bf16[128,1024]{1,0:T(8,128)(2,1)S(1)}, u32[]{:S(2)}, u32[]{:S(2)}) %collective-permute-start) | collective-permute-done | bytes 262176 | tf_op jit(solution)/shard_map/ppermute | solution.py:22
  100.7 0.0 copy-start
  100.7 1.2 copy-done
  101.9 0.0 copy-start.1
  101.9 1.2 copy-done.1
  103.1 0.0 copy-start.2
  103.1 1.2 copy-done.2
  104.3 0.0 copy-start.5
  104.3 0.9 copy-done.5
  105.3 0.0 copy-start.6
  105.3 0.9 copy-done.6
  106.2 0.0 copy-start.7
  106.2 0.9 copy-done.7
  107.1 0.0 copy-start.8
  107.1 0.8 copy-done.8
  107.9 0.0 copy-start.9
  107.9 0.8 copy-done.9
  108.8 0.0 copy-start.3
  108.8 0.0 copy-start.4
  108.8 5.1 %shard_map.122.hyena_ref = bf16[512,1024]{1,0:T(8,128)(2,1)} custom-call(bf16[128,1024]{1,0:T(8,128)(2,1)S(1)} %collective-permute-done.rim_ref, bf16[512,1024]{1,0:T(8,128)(2,1)S(1)} %copy-done.2, bf16[512,1024]{1,0:T(8,128)(2,1)S(1)} %copy-done.1, bf16[512,1024]{1,0:T(8,128)(2,1)S(1)} %copy-done, bf16[128,1024]{1,0:T(8,128)(2,1)S(1)} %copy-done.5, ...), custom_call_target="tpu_custom_call" | custom-call | flops 3000000000 | bytes 5242880 | tf_op jit(solution)/shard_map/pallas_call | solution.py:81
  113.9 0.1 copy.14.start_ref
  114.0 0.0 collective-permute-done.2.refs_2_
  114.1 0.0 collective-permute-done.4.refs_5_
  114.1 0.0 copy-done.3
  114.1 0.0 copy-done.4
  114.1 13.2 %shard_map.123.attended_ref = bf16[512,1024]{1,0:T(8,128)(2,1)S(1)} custom-call(s32[512,1]{1,0:T(8,128)S(1)} %copy.14.start_ref, bf16[512,1024]{1,0:T(8,128)(2,1)S(1)} %copy-done.3, bf16[512,1024]{1,0:T(8,128)(2,1)S(1)} %copy-done.4, bf16[512,1024]{1,0:T(8,128)(2,1)S(1)} %collective-permute-done.1.refs_1_, bf16[512,1024]{1,0:T(8,128)(2,1)} %collective-permute-done.2.refs_2_, ...), custom_call_target="tpu_custom_call" | custom-call | flops 4000000000 | bytes 8388608 | tf_op jit(solution)/shard_map/pallas_call | solution.py:127
  127.3 0.0 copy-start.10
  127.3 1.0 copy-done.10
  128.3 50.8 %shard_map.124 = bf16[512,1024]{1,0:T(8,128)(2,1)} custom-call(bf16[512,1024]{1,0:T(8,128)(2,1)} %copy-done.10, bf16[512,1024]{1,0:T(8,128)(2,1)} %shard_map.122.hyena_ref, bf16[1024,8192]{1,0:T(8,128)(2,1)} %weight_ref.1), custom_call_target="tpu_custom_call" | custom-call | flops 8999999488 | bytes 20971520 | tf_op jit(solution)/shard_map/pallas_call | solution.py:261
  179.1 2.3 %copy.16 = bf16[512,1024]{1,0:T(8,128)(2,1)} copy(bf16[512,1024]{1,0:T(8,128)(2,1)} %shard_map.124) | data formatting | bytes 2097152
  (1 shorter events, 0.0 us)
Async XLA Ops:
  0.6 28.2 %collective-permute-start.1 = (bf16[512,1024]{1,0:T(8,128)(2,1)}, bf16[512,1024]{1,0:T(8,128)(2,1)S(1)}, u32[]{:S(2)}, u32[]{:S(2)}) collective-permute-start(bf16[512,1024]{1,0:T(8,128)(2,1)} %refs_0_.1), channel_id=1, source_target_pairs={{0,8},{8,16},{16,24},{1,9},{9,17},{17,25},{2,10},{10,18},{18,26},{... | collective-permute-start | bytes 3145736 | tf_op jit(solution)/shard_map/ppermute | solution.py:22
  4.1 47.2 %collective-permute-start.3 = (bf16[512,1024]{1,0:T(8,128)(2,1)}, bf16[512,1024]{1,0:T(8,128)(2,1)}, u32[]{:S(2)}, u32[]{:S(2)}) collective-permute-start(bf16[512,1024]{1,0:T(8,128)(2,1)} %refs_3_.1), channel_id=1, source_target_pairs={{0,8},{8,16},{16,24},{1,9},{9,17},{17,25},{2,10},{10,18},{18,26},{... | collective-permute-start | bytes 3145736 | tf_op jit(solution)/shard_map/ppermute | solution.py:22
  28.8 85.3 %collective-permute-start.2 = (bf16[512,1024]{1,0:T(8,128)(2,1)S(1)}, bf16[512,1024]{1,0:T(8,128)(2,1)}, u32[]{:S(2)}, u32[]{:S(2)}) collective-permute-start(bf16[512,1024]{1,0:T(8,128)(2,1)S(1)} %collective-permute-done.1.refs_1_), channel_id=1, source_target_pairs={{0,8},{8,16},{16,24},{1,9},{9,17},{17,25},{2,10},{10,18},{18,26},{... | collective-permute-start | bytes 3145736 | tf_op jit(solution)/shard_map/ppermute | solution.py:22
  51.4 62.7 %collective-permute-start.4 = (bf16[512,1024]{1,0:T(8,128)(2,1)}, bf16[512,1024]{1,0:T(8,128)(2,1)}, u32[]{:S(2)}, u32[]{:S(2)}) collective-permute-start(bf16[512,1024]{1,0:T(8,128)(2,1)} %collective-permute-done.3.refs_4_), channel_id=1, source_target_pairs={{0,8},{8,16},{16,24},{1,9},{9,17},{17,25},{2,10},{10,18},{18,26},{... | collective-permute-start | bytes 3145736 | tf_op jit(solution)/shard_map/ppermute | solution.py:22
  55.9 44.7 %collective-permute-start = (bf16[128,1024]{1,0:T(8,128)(2,1)S(1)}, bf16[128,1024]{1,0:T(8,128)(2,1)S(1)}, u32[]{:S(2)}, u32[]{:S(2)}) collective-permute-start(bf16[128,1024]{1,0:T(8,128)(2,1)S(1)} %multiply_convert_fusion), channel_id=1, source_target_pairs={{0,8},{8,16},{16,24},{1,9},{9,17},{17,25},{2,10},{10,18},{18,26},{... | collective-permute-start | bytes 786440 | tf_op jit(solution)/shard_map/ppermute | solution.py:22
  100.7 1.2 copy-start
  101.9 1.2 copy-start.1
  103.1 1.2 copy-start.2
  104.3 0.9 copy-start.5
  105.3 0.9 copy-start.6
  106.2 0.9 copy-start.7
  107.1 0.8 copy-start.8
  107.9 0.8 copy-start.9
  108.8 5.3 %copy-start.3 = (bf16[512,1024]{1,0:T(8,128)(2,1)S(1)}, bf16[512,1024]{1,0:T(8,128)(2,1)}, u32[]{:S(2)}) copy-start(bf16[512,1024]{1,0:T(8,128)(2,1)} %query_ref.3) | copy-start | bytes 3145732
  108.8 5.3 %copy-start.4 = (bf16[512,1024]{1,0:T(8,128)(2,1)S(1)}, bf16[512,1024]{1,0:T(8,128)(2,1)}, u32[]{:S(2)}) copy-start(bf16[512,1024]{1,0:T(8,128)(2,1)} %refs_0_.1) | copy-start | bytes 3145732
  127.3 1.0 copy-start.10

commit v2 on v1

v2 whole, which is shorter than its diff:
```python
import functools

import jax
import jax.numpy as jnp
import numpy as np
from jax import lax
from jax.experimental import pallas as pl
from jax.experimental.pallas import tpu as pltpu
from jax.sharding import PartitionSpec as P

HEAD_DIM = 128
LOG2_E = 1.4426950408889634
CHANNEL_TILE = 256
MIX_ROWS = 128
MESH = pl.DeviceIdType.MESH


def shifted(x, axis, by):
    devices = lax.axis_size(axis)
    pairs = [(i, i + by) for i in range(devices) if 0 <= i + by < devices]
    return lax.ppermute(x, axis, pairs)


def split_high_low(matrix):
    exact = jnp.asarray(matrix, jnp.float32)
    high = exact.astype(jnp.bfloat16)
    low = (exact - high.astype(jnp.float32)).astype(jnp.bfloat16)
    return high, low


def fourier_matrices(taps):
    size = 2 * taps
    n = np.arange(size)
    k = np.arange(taps)
    angle = 2.0 * np.pi * np.outer(k, n) / size
    alternating = np.where(n % 2 == 0, 1.0, -1.0)
    forward = np.concatenate([np.cos(angle), alternating[None], np.sin(angle)[1:]], axis=0)
    gain = np.full((size,), 2.0 / size)
    gain[0] = gain[taps] = 1.0 / size
    inverse = (forward * gain[:, None]).T[taps:]
    return forward.astype(np.float32), inverse.astype(np.float32)


def dot32(a, b):
    return jnp.dot(a, b, preferred_element_type=jnp.float32)


def hyena_kernel(
    rim_ref, query_ref, key_ref, value_ref, taps_ref, projected_ref, fh_ref, fl_ref, gh_ref, gl_ref, out_ref, stream_ref
):
    rows, _ = key_ref.shape
    taps = taps_ref.shape[0]
    fh, fl, gh, gl = fh_ref[...], fl_ref[...], gh_ref[...], gl_ref[...]
    tap_freq = dot32(fh[:, :taps], taps_ref[...]) + dot32(fl[:, :taps], taps_ref[...])
    tap_cos, tap_sin = tap_freq[:taps], tap_freq[taps:]
    edge = lax.broadcasted_iota(jnp.int32, tap_cos.shape, 0) == 0
    before = rim_ref[...]
    for block in range(rows // taps):
        here = slice(block * taps, (block + 1) * taps)
        now = (key_ref[here, :].astype(jnp.float32) * value_ref[here, :].astype(jnp.float32)).astype(jnp.bfloat16)
        window = jnp.concatenate([before, now], axis=0)
        freq = dot32(fh, window) + dot32(fl, window)
        cos, sin = freq[:taps], freq[taps:]
        sin_sin = sin * tap_sin
        real = cos * tap_cos - jnp.where(edge, 0.0, sin_sin)
        imag = jnp.where(edge, sin_sin, cos * tap_sin + sin * tap_cos)
        product = jnp.concatenate([real, imag], axis=0)
        high = product.astype(jnp.bfloat16)
        low = (product - high.astype(jnp.float32)).astype(jnp.bfloat16)
        filtered = dot32(gh, high) + dot32(gh, low) + dot32(gl, high)
        hyena_out = (query_ref[here, :].astype(jnp.float32) * filtered).astype(jnp.bfloat16)
        out_ref[here, :] = hyena_out
        stream_ref[here, :] = (hyena_out.astype(jnp.float32) + projected_ref[here, :]).astype(jnp.bfloat16)
        before = now


def hyena(rim, query, key, value, taps, projected):
    rows, width = key.shape
    tap_count = taps.shape[0]
    forward, inverse = fourier_matrices(tap_count)
    constants = split_high_low(forward) + split_high_low(inverse)
    column = lambda r: pl.BlockSpec((r, CHANNEL_TILE), lambda i: (0, i))
    whole = lambda a: pl.BlockSpec(a.shape, lambda i: (0, 0))
    return pl.pallas_call(
        hyena_kernel,
        out_shape=[jax.ShapeDtypeStruct((rows, width), jnp.bfloat16)] * 2,
        grid=(width // CHANNEL_TILE,),
        in_specs=[column(tap_count), column(rows), column(rows), column(rows), column(tap_count), column(rows)]
        + [whole(a) for a in constants],
        out_specs=[column(rows)] * 2,
        compiler_params=pltpu.CompilerParams(vmem_limit_bytes=48 * 2**20),
        cost_estimate=pl.CostEstimate(flops=3 * 10**9, bytes_accessed=5 * 2**20, transcendentals=0),
    )(rim, query, key, value, taps, projected, *constants)


def spread_exactly(value, lane, head, heads, into):
    high = value.astype(jnp.bfloat16).astype(jnp.float32)
    middle = (value - high).astype(jnp.bfloat16).astype(jnp.float32)
    low = value - high - middle
    into = jnp.where(lane == head, high, into)
    into = jnp.where(lane == head + heads, middle, into)
    return jnp.where(lane == head + 2 * heads, low, into)


def gathered(stats, lane, head, heads):
    wanted = (lane == head) | (lane == head + heads) | (lane == head + 2 * heads)
    return jnp.sum(jnp.where(wanted, stats, 0.0), axis=1, keepdims=True)


def head_columns(head):
    return pl.ds(pl.multiple_of(head * HEAD_DIM, HEAD_DIM), HEAD_DIM)


def mix_kernel(
    devices,
    n,
    chunk,
    start_ref,
    query_ref,
    key_ref,
    value_ref,
    weight_ref,
    out_ref,
    query_in,
    parts_own,
    parts_in,
    attended_ref,
    weights,
    away,
    near,
    landed,
    query_send,
    query_recv,
    parts_send,
    parts_recv,
    load_sem,
    send_sem,
    recv_sem,
):
    rows, width = out_ref.shape
    chunks = rows // chunk
    stages = n.bit_length() - 1
    hops = devices // 2
    heads = width // HEAD_DIM
    scale = HEAD_DIM ** (-0.5) * LOG2_E
    place = lax.axis_index("ctx")
    me = lax.axis_index("head")
    core = me % 2

    def flip(bit, by):
        return bit + by - 2 * bit * by

    def slot_bit(slot, stage):
        return (slot // (n >> (stage + 1))) % 2

    def destination(slot):
        to_core = flip(core, slot_bit(slot, 0))
        target = to_core
        for axis in range(1, stages):
            across = slot_bit(slot, axis) * (1 - to_core) + slot_bit(slot, stages - axis) * to_core
            target = target + flip((me // 2**axis) % 2, across) * 2**axis
        return target

    def partner(stage):
        if stage == 0:
            return me + 1 - 2 * core
        forward = me + (1 - 2 * ((me // 2**stage) % 2)) * 2**stage
        other = stages - stage
        backward = me + (1 - 2 * ((me // 2**other) % 2)) * 2**other
        return forward * (1 - core) + backward * core

    loads = []
    for slot in list(range(n // 2, n)) + list(range(n // 2)):
        columns = pl.ds(pl.multiple_of(destination(slot) * width, width), width)
        load = pltpu.make_async_copy(weight_ref.at[:, columns], weights.at[slot], load_sem.at[slot])
        load.start()
        loads.append((slot, load))

    barrier = pltpu.get_barrier_semaphore()
    for stage in range(stages):
        pl.semaphore_signal(barrier, inc=1, device_id={"head": partner(stage)}, device_id_type=MESH)

    @pl.when(place > 0)
    def _():
        pl.semaphore_signal(barrier, inc=1, device_id={"ctx": place - 1}, device_id_type=MESH)

    @pl.when(place < devices - 1)
    def _():
        pl.semaphore_signal(barrier, inc=1, device_id={"ctx": place + 1}, device_id_type=MESH)

    has_lower = (place + devices - 1) // devices
    has_upper = 1 - place // (devices - 1)
    pl.semaphore_wait(barrier, stages + has_lower + has_upper)

    def rows_of(part):
        return pl.ds(part * chunk, chunk)

    def query_copy(distance, part):
        source = query_ref if distance == 0 else query_in.at[distance - 1]
        return pltpu.make_async_remote_copy(
            src_ref=source.at[rows_of(part)],
            dst_ref=query_in.at[distance, rows_of(part)],
            send_sem=query_send.at[distance, part],
            recv_sem=query_recv.at[distance, part],
            device_id={"ctx": place - 1},
            device_id_type=MESH,
        )

    def parts_copy(distance, part):
        return pltpu.make_async_remote_copy(
            src_ref=parts_own.at[distance, rows_of(part)],
            dst_ref=parts_in.at[distance - 1, rows_of(part)],
            send_sem=parts_send.at[distance - 1, part],
            recv_sem=parts_recv.at[distance - 1, part],
            device_id={"ctx": place + 1},
            device_id_type=MESH,
        )

    def in_window(distance):
        return place + distance < devices

    def attend(distance, part):
        first = part * chunk if distance == hops else 0
        last = (part + 1) * chunk if distance == 0 else rows
        queries = query_ref if distance == 0 else query_in.at[distance - 1]
        lane = lax.broadcasted_iota(jnp.int32, (chunk, HEAD_DIM), 1)

        def one_head(head, stats):
            columns = head_columns(head)
            scores = lax.dot_general(
                queries[rows_of(part), columns],
                key_ref[first:last, columns],
                (((1,), (1,)), ((), ())),
                preferred_element_type=jnp.float32,
            )
            position = lax.broadcasted_iota(jnp.int32, scores.shape, 1) + (first - distance * rows)
            allowed = position >= start_ref[distance, rows_of(part), :]
            if distance == 0:
                allowed &= position <= lax.broadcasted_iota(jnp.int32, scores.shape, 0) + part * chunk
            scores = jnp.where(allowed, scores, -1e30)
            top = jnp.max(scores, axis=1, keepdims=True)
            probs = jnp.exp2((scores - top) * scale)
            total = jnp.sum(probs, axis=1, keepdims=True)
            weighted = dot32(probs.astype(jnp.bfloat16), value_ref[first:last, columns])
            parts_own[distance, rows_of(part), columns] = (weighted / total).astype(jnp.bfloat16)
            return spread_exactly(top * scale + jnp.log(total) * LOG2_E, lane, head, heads, stats)

        stats = lax.fori_loop(0, heads, one_head, jnp.zeros((chunk, HEAD_DIM), jnp.float32), unroll=2)
        parts_own[distance, rows_of(part), width:] = stats.astype(jnp.bfloat16)

    def merge(distance, part):
        lane = lax.broadcasted_iota(jnp.int32, (chunk, HEAD_DIM), 1)
        own_stats = parts_own[distance, rows_of(part), width:].astype(jnp.float32)
        in_stats = parts_in[distance, rows_of(part), width:].astype(jnp.float32)

        def one_head(head, stats):
            columns = head_columns(head)
            own, arrived = gathered(own_stats, lane, head, heads), gathered(in_stats, lane, head, heads)
            top = jnp.maximum(own, arrived)
            own_share, in_share = jnp.exp2(own - top), jnp.exp2(arrived - top)
            total = own_share + in_share
            merged = (
                parts_own[distance, rows_of(part), columns].astype(jnp.float32) * (own_share / total)
                + parts_in[distance, rows_of(part), columns].astype(jnp.float32) * (in_share / total)
            ).astype(jnp.bfloat16)
            if distance == 0:
                attended_ref[rows_of(part), columns] = merged
                return stats
            parts_own[distance, rows_of(part), columns] = merged
            return spread_exactly(top + jnp.log(total) * LOG2_E, lane, head, heads, stats)

        stats = lax.fori_loop(0, heads, one_head, jnp.zeros((chunk, HEAD_DIM), jnp.float32), unroll=2)
        if distance > 0:
            parts_own[distance, rows_of(part), width:] = stats.astype(jnp.bfloat16)

    def send_own_queries(part):
        @pl.when(place > 0)
        def _():
            query_copy(0, part).start()

    def near_distances(part):
        attend(0, part)
        for distance in range(1, hops):

            @pl.when(in_window(distance))
            def _():
                query_copy(distance - 1, part).wait_recv()

                @pl.when(place > 0)
                def _():
                    query_copy(distance, part).start()

        if part + 2 < chunks:
            send_own_queries(part + 2)
        for distance in range(1, hops):

            @pl.when(in_window(distance))
            def _():
                attend(distance, part)

                @pl.when(place == 0)
                def _():
                    parts_copy(distance, part).start()

    def far_distance(part):
        @pl.when(in_window(hops))
        def _():
            query_copy(hops - 1, part).wait_recv()
            attend(hops, part)
            parts_copy(hops, part).start()

    def merge_all(part):
        @pl.when(place > 0)
        def _():
            for distance in range(hops - 1, -1, -1):

                @pl.when(in_window(distance))
                def _():
                    parts_copy(distance + 1, part).wait_recv()
                    merge(distance, part)
                    if distance > 0:
                        parts_copy(distance, part).start()

        @pl.when(place == 0)
        def _():
            attended_ref[rows_of(part), :] = parts_own[0, rows_of(part), :width]

    first_of = [n - (n >> stage) for stage in range(stages)]

    def copy(stage, part):
        count = n >> (stage + 1)
        source = away.at[part] if stage == 0 else near.at[part, pl.ds(count, count)]
        return pltpu.make_async_remote_copy(
            src_ref=source,
            dst_ref=landed.at[part, pl.ds(first_of[stage], count)],
            send_sem=send_sem.at[stage, part],
            recv_sem=recv_sem.at[stage, part],
            device_id={"head": partner(stage)},
            device_id_type=MESH,
        )

    def term(part, slot):
        return jnp.dot(
            attended_ref[part * chunk : (part + 1) * chunk, :], weights[slot], preferred_element_type=jnp.float32
        )

    def far_terms(part):
        if part == 0:
            for _, load in loads[: n // 2]:
                load.wait()

        @pl.loop(0, n // 2)
        def _(index):
            away[part, index] = term(part, index + n // 2).astype(jnp.bfloat16)

        copy(0, part).start()

    def near_terms(part):
        if part == 0:
            for _, load in loads[n // 2 :]:
                load.wait()
        copy(0, part).wait_recv()

        def add(index):
            total = term(part, index) + landed[part, index].astype(jnp.float32)
            near[part, index] = total.astype(jnp.bfloat16)

        pl.loop(n // 4, n // 2)(add)
        copy(1, part).start()
        pl.loop(0, n // 4)(add)

    def fold(stage, part):
        copy(stage, part).wait_recv()
        half = n >> (stage + 2)

        def add(index):
            arrived = landed[part, first_of[stage] + index].astype(jnp.float32)
            near[part, index] = (near[part, index].astype(jnp.float32) + arrived).astype(jnp.bfloat16)

        pl.loop(half, 2 * half)(add)
        copy(stage + 1, part).start()
        pl.loop(0, half)(add)

    def finish(part):
        last = stages - 1
        copy(last, part).wait_recv()
        out_ref[part * chunk : (part + 1) * chunk, :] = near[part, 0].astype(jnp.float32) + landed[
            part, first_of[last]
        ].astype(jnp.float32)

    send_own_queries(0)
    if chunks > 1:
        send_own_queries(1)
    for step in range(chunks + stages + 2):
        if step < chunks:
            near_distances(step)
        if 0 <= step - 1 < chunks:
            far_distance(step - 1)
        if 0 <= step - 2 < chunks:
            merge_all(step - 2)
            far_terms(step - 2)
        for stage in range(1, stages):
            if 0 <= step - 2 - stage < chunks:
                near_terms(step - 3) if stage == 1 else fold(stage - 1, step - 2 - stage)
        if 0 <= step - 2 - stages < chunks:
            finish(step - 2 - stages)
    for part in range(chunks):
        for stage in range(stages):
            copy(stage, part).wait_send()
        for distance in range(hops):

            @pl.when((place > 0) & in_window(distance))
            def _():
                query_copy(distance, part).wait_send()

            @pl.when(in_window(distance + 1))
            def _():
                parts_copy(distance + 1, part).wait_send()


def mix(start, query, key, value, weight):
    rows, width = query.shape
    devices, n = lax.axis_size("ctx"), lax.axis_size("head")
    hops = devices // 2
    chunks = rows // MIX_ROWS
    stages = n.bit_length() - 1
    vmem = pl.BlockSpec(memory_space=pltpu.VMEM)
    return pl.pallas_call(
        functools.partial(mix_kernel, devices, n, MIX_ROWS),
        out_shape=jax.ShapeDtypeStruct((rows, width), jnp.float32),
        in_specs=[vmem] * 4 + [pl.BlockSpec(memory_space=pl.ANY)],
        out_specs=vmem,
        scratch_shapes=[
            pltpu.VMEM((hops, rows, width), jnp.bfloat16),
            pltpu.VMEM((hops + 1, rows, width + HEAD_DIM), jnp.bfloat16),
            pltpu.VMEM((hops, rows, width + HEAD_DIM), jnp.bfloat16),
            pltpu.VMEM((rows, width), jnp.bfloat16),
            pltpu.VMEM((n, width, width), jnp.bfloat16),
            pltpu.VMEM((chunks, n // 2, MIX_ROWS, width), jnp.bfloat16),
            pltpu.VMEM((chunks, n // 2, MIX_ROWS, width), jnp.bfloat16),
            pltpu.VMEM((chunks, n - 1, MIX_ROWS, width), jnp.bfloat16),
            pltpu.SemaphoreType.DMA((hops, chunks)),
            pltpu.SemaphoreType.DMA((hops, chunks)),
            pltpu.SemaphoreType.DMA((hops, chunks)),
            pltpu.SemaphoreType.DMA((hops, chunks)),
            pltpu.SemaphoreType.DMA((n,)),
            pltpu.SemaphoreType.DMA((stages, chunks)),
            pltpu.SemaphoreType.DMA((stages, chunks)),
        ],
        compiler_params=pltpu.CompilerParams(
            collective_id=0, has_side_effects=True, vmem_limit_bytes=60 * 2**20
        ),
        cost_estimate=pl.CostEstimate(flops=13 * 10**9, bytes_accessed=24 * 2**20, transcendentals=6 * 10**6),
    )(start, query, key, value, weight)


def on_device(
    hyena_query,
    hyena_key,
    hyena_value,
    hyena_filter,
    attn_query,
    attn_key,
    attn_value,
    segment_ids,
    out_weight,
):
    num_rows = hyena_key.shape[0]
    tap_count = hyena_filter.shape[0]
    hops = lax.axis_size("ctx") // 2
    last_key = hyena_key[num_rows - tap_count :].astype(jnp.float32)
    last_value = hyena_value[num_rows - tap_count :].astype(jnp.float32)
    rim = shifted((last_key * last_value).astype(jnp.bfloat16), "ctx", 1)
    devices = lax.axis_size("ctx")
    document_start = []
    for distance in range(hops + 1):
        offset = jnp.minimum(lax.axis_index("ctx") + distance, devices - 1) * num_rows
        segments = lax.dynamic_slice_in_dim(segment_ids, offset, num_rows)
        earlier = jnp.sum((segment_ids[None, :] < segments[:, None]).astype(jnp.int32), axis=1)
        document_start.append(earlier - offset)
    start = jnp.stack(document_start)[..., None]
    projected = mix(start, attn_query, attn_key, attn_value, out_weight)
    hyena_out, stream = hyena(rim, hyena_query, hyena_key, hyena_value, hyena_filter, projected)
    return (hyena_out, stream)


def solution(mesh):
    return jax.shard_map(
        on_device,
        mesh=mesh,
        in_specs=(
            P("ctx", "head"),
            P("ctx", "head"),
            P("ctx", "head"),
            P(None, "head"),
            P("ctx", "head"),
            P("ctx", "head"),
            P("ctx", "head"),
            P(),
            P("head", None),
        ),
        out_specs=(P("ctx", "head"), P("ctx", "head")),
        check_vma=False,
    )
```

time: 183 us -> 137 us (0.75)
  waiting for transfers between devices: 82.6 us -> 0.01 us
  Pallas kernels: 69.1 us -> 123 us
  starting transfers between devices: 14.3 us -> 3.47 us
  local copies, waits for them, and re-layouts: 12.3 us -> 3.69 us
    ppermute x5 -> x1, waiting for transfers between devices: 82.6 us -> 0.01 us  [shifted(): return lax.ppermute(x, axis, pairs)]
    pallas_call x3 -> x2, Pallas kernels: 69.1 us -> 123 us  [the longest x1 117 us: mix(): pl.pallas_call(functools.partial(mix_kernel, devices, n, MIX_ROWS), out_s...]
    ppermute x5 -> x1, starting transfers between devices: 14.3 us -> 3.47 us  [shifted(): return lax.ppermute(x, axis, pairs)]
    unnamed x23 -> x18, local copies, waits for them, and re-layouts: 11.3 us -> 1.63 us
  transfers between devices with their start and end apart: 5 -> 1, of which waited for: 3 -> 0; matrix products, arithmetic and copies ran while one was open for 2% -> 3% of each run, Pallas kernels for 3% -> 87%
where the time goes in v2:
time: 137 us; the launch traced here: 135 us
  Pallas kernels  123 us (90%)
  other arithmetic  4.04 us (3%)
  local copies, waits for them, and re-layouts  3.69 us (3%)
  starting transfers between devices  3.47 us (3%)
    pallas_call x1, Pallas kernels, mix(): pl.pallas_call(functools.partial(mix_kernel, devices, n, MIX_ROWS), out_s...  117 us
    pallas_call x1, Pallas kernels, hyena(): pl.pallas_call(hyena_kernel, out_shape=[jax.ShapeDtypeStruct((rows, width...  5.4 us
    ppermute x1, starting transfers between devices, shifted(): return lax.ppermute(x, axis, pairs)  3.47 us
  transfers between devices with their start and end apart: 1, of which 0 were waited for; matrix products, arithmetic and copies ran while one was open for 3% of the time, Pallas kernels for 87%

profile of v2, /device:TPU:16, one launch (start us, length us, event | category | flops | bytes accessed | tf_op | source)
XLA Modules:
  0.0 134.9 jit_solution(3219893827684766772)
XLA Ops:
  0.6 1.8 %multiply_convert_fusion = bf16[128,1024]{1,0:T(8,128)(2,1)} fusion(bf16[512,1024]{1,0:T(8,128)(2,1)} %value_ref.3, bf16[512,1024]{1,0:T(8,128)(2,1)} %key_ref.3), kind=kLoop, calls=%fused_computation.3 | loop fusion | flops 524288 | bytes 786432 | tf_op jit(solution)/shard_map/convert_element_type | solution.py:473
  2.4 3.5 %collective-permute-start = (bf16[128,1024]{1,0:T(8,128)(2,1)}, bf16[128,1024]{1,0:T(8,128)(2,1)S(1)}, u32[]{:S(2)}, u32[]{:S(2)}) collective-permute-start(bf16[128,1024]{1,0:T(8,128)(2,1)} %multiply_convert_fusion), channel_id=1, source_target_pairs={{0,8},{8,16},{16,24},{1,9},{9,17},{17,25},{2,10},{10,18},{18,26},{... | collective-permute-start | bytes 786440 | tf_op jit(solution)/shard_map/ppermute | solution.py:21
  5.9 0.9 fusion
  6.8 2.2 %convert_reduce_fusion.2 = (s32[512]{0:T(512)S(1)}, s32[512]{0:T(512)S(1)}, s32[512]{0:T(512)S(1)}) fusion(s32[2048]{0:T(1024)} %param.18, s32[512]{0:T(512)S(1)} %get-tuple-element.6, s32[512]{0:T(512)S(1)} %get-tuple-element.7, s32[512]{0:T(512)S(1)} %get-tuple-element.5), kind=kLoop, calls=%fused_computation.2 | loop fusion | flops 9435648 | bytes 20480 | tf_op jit(solution)/shard_map/reduce_sum | solution.py:479
  9.1 1.2 copy.14.start_ref
  10.2 0.0 copy-start
  10.3 0.0 copy-start.1
  10.3 0.0 copy-start.2
  10.3 0.0 copy-start.3
  10.3 0.0 copy-start.4
  10.3 0.0 copy-start.5
  10.3 0.0 copy-start.6
  10.3 0.0 copy-start.7
  10.3 117.5 %shard_map.122.projected_ref = f32[512,1024]{1,0:T(8,128)} custom-call(s32[3,512,1]{2,1,0:T(8,128)} %copy.14.start_ref, bf16[512,1024]{1,0:T(8,128)(2,1)} %query_ref.2, bf16[512,1024]{1,0:T(8,128)(2,1)} %key_ref.2, bf16[512,1024]{1,0:T(8,128)(2,1)} %value_ref.2, bf16[1024,8192]{1,0:T(8,128)(2,1)} %weight_ref.1), custom_call_target="tpu_custom_call" | custom-call | flops 12999999488 | bytes 25165824 | tf_op jit(solution)/shard_map/pallas_call | solution.py:428
  127.8 0.0 collective-permute-done.rim_ref
  127.8 0.0 copy-done
  127.8 0.0 copy-done.1
  127.8 0.0 copy-done.2
  127.8 0.0 copy-done.3
  127.8 0.0 copy-done.4
  127.8 0.0 copy-done.5
  127.8 0.0 copy-done.6
  127.9 0.0 copy-done.7
  127.9 0.0 copy-start.8
  127.9 1.6 %copy-done.8 = f32[512,1024]{1,0:T(8,128)S(1)} copy-done((f32[512,1024]{1,0:T(8,128)S(1)}, f32[512,1024]{1,0:T(8,128)}, u32[]{:S(2)}) %copy-start.8) | copy-done | bytes 2097176
  129.5 5.4 %shard_map.123 = (bf16[512,1024]{1,0:T(8,128)(2,1)}, bf16[512,1024]{1,0:T(8,128)(2,1)}) custom-call(bf16[128,1024]{1,0:T(8,128)(2,1)S(1)} %collective-permute-done.rim_ref, bf16[512,1024]{1,0:T(8,128)(2,1)S(1)} %copy-done.2, bf16[512,1024]{1,0:T(8,128)(2,1)S(1)} %copy-done.1, bf16[512,1024]{1,0:T(8,128)(2,1)S(1)} %copy-done, ...), custom_call_target="tpu_custom_call" | custom-call | flops 3000000000 | bytes 5242880 | tf_op jit(solution)/shard_map/pallas_call | solution.py:84
  (3 shorter events, 0.0 us)
Async XLA Ops:
  2.4 125.3 %collective-permute-start = (bf16[128,1024]{1,0:T(8,128)(2,1)}, bf16[128,1024]{1,0:T(8,128)(2,1)S(1)}, u32[]{:S(2)}, u32[]{:S(2)}) collective-permute-start(bf16[128,1024]{1,0:T(8,128)(2,1)} %multiply_convert_fusion), channel_id=1, source_target_pairs={{0,8},{8,16},{16,24},{1,9},{9,17},{17,25},{2,10},{10,18},{18,26},{... | collective-permute-start | bytes 786440 | tf_op jit(solution)/shard_map/ppermute | solution.py:21
  10.2 117.5 %copy-start = (bf16[512,1024]{1,0:T(8,128)(2,1)S(1)}, bf16[512,1024]{1,0:T(8,128)(2,1)}, u32[]{:S(2)}) copy-start(bf16[512,1024]{1,0:T(8,128)(2,1)} %value_ref.3) | copy-start | bytes 3145732
  10.3 117.5 %copy-start.1 = (bf16[512,1024]{1,0:T(8,128)(2,1)S(1)}, bf16[512,1024]{1,0:T(8,128)(2,1)}, u32[]{:S(2)}) copy-start(bf16[512,1024]{1,0:T(8,128)(2,1)} %key_ref.3) | copy-start | bytes 3145732
  10.3 117.5 %copy-start.2 = (bf16[512,1024]{1,0:T(8,128)(2,1)S(1)}, bf16[512,1024]{1,0:T(8,128)(2,1)}, u32[]{:S(2)}) copy-start(bf16[512,1024]{1,0:T(8,128)(2,1)} %query_ref.3) | copy-start | bytes 3145732
  10.3 117.6 %copy-start.3 = (bf16[128,1024]{1,0:T(8,128)(2,1)S(1)}, bf16[128,1024]{1,0:T(8,128)(2,1)}, u32[]{:S(2)}) copy-start(bf16[128,1024]{1,0:T(8,128)(2,1)} %taps_ref.1) | copy-start | bytes 786436
  10.3 117.6 %copy-start.4 = (bf16[256,256]{1,0:T(8,128)(2,1)S(1)}, bf16[256,256]{1,0:T(8,128)(2,1)}, u32[]{:S(2)}) copy-start(bf16[256,256]{1,0:T(8,128)(2,1)} %constant.26.fl_ref) | copy-start | bytes 393220
  10.3 117.6 %copy-start.5 = (bf16[256,256]{1,0:T(8,128)(2,1)S(1)}, bf16[256,256]{1,0:T(8,128)(2,1)}, u32[]{:S(2)}) copy-start(bf16[256,256]{1,0:T(8,128)(2,1)} %constant.23.fh_ref) | copy-start | bytes 393220
  10.3 117.6 %copy-start.6 = (bf16[128,256]{1,0:T(8,128)(2,1)S(1)}, bf16[128,256]{1,0:T(8,128)(2,1)}, u32[]{:S(2)}) copy-start(bf16[128,256]{1,0:T(8,128)(2,1)} %constant.30.gl_ref) | copy-start | bytes 196612
  10.3 117.6 %copy-start.7 = (bf16[128,256]{1,0:T(8,128)(2,1)S(1)}, bf16[128,256]{1,0:T(8,128)(2,1)}, u32[]{:S(2)}) copy-start(bf16[128,256]{1,0:T(8,128)(2,1)} %constant.27.gh_ref) | copy-start | bytes 196612
  127.9 1.6 %copy-start.8 = (f32[512,1024]{1,0:T(8,128)S(1)}, f32[512,1024]{1,0:T(8,128)}, u32[]{:S(2)}) copy-start(f32[512,1024]{1,0:T(8,128)} %shard_map.122.projected_ref) | copy-start | bytes 6291460

commit v3 on v2

--- a/solution.py
+++ b/solution.py
@@ -115,6 +115,7 @@
     devices,
     n,
     chunk,
+    far_place,
     start_ref,
     query_ref,
     key_ref,
@@ -219,6 +220,9 @@
     def in_window(distance):
         return place + distance < devices
 
+    def reaches_below(distance):
+        return place == far_place + 1 if distance == hops - 1 else (place > 0) & in_window(distance)
+
     def attend(distance, part):
         first = part * chunk if distance == hops else 0
         last = (part + 1) * chunk if distance == 0 else rows
@@ -286,7 +290,7 @@
             def _():
                 query_copy(distance - 1, part).wait_recv()
 
-                @pl.when(place > 0)
+                @pl.when(reaches_below(distance))
                 def _():
                     query_copy(distance, part).start()
 
@@ -298,28 +302,26 @@
             def _():
                 attend(distance, part)
 
-                @pl.when(place == 0)
+                @pl.when(place != far_place + 1 if distance == hops - 1 else place == 0)
                 def _():
                     parts_copy(distance, part).start()
 
     def far_distance(part):
-        @pl.when(in_window(hops))
+        @pl.when(place == far_place)
         def _():
             query_copy(hops - 1, part).wait_recv()
             attend(hops, part)
             parts_copy(hops, part).start()
 
     def merge_all(part):
-        @pl.when(place > 0)
-        def _():
-            for distance in range(hops - 1, -1, -1):
-
-                @pl.when(in_window(distance))
-                def _():
-                    parts_copy(distance + 1, part).wait_recv()
-                    merge(distance, part)
-                    if distance > 0:
-                        parts_copy(distance, part).start()
+        for distance in range(hops - 1, -1, -1):
+
+            @pl.when(reaches_below(distance))
+            def _():
+                parts_copy(distance + 1, part).wait_recv()
+                merge(distance, part)
+                if distance > 0:
+                    parts_copy(distance, part).start()
 
         @pl.when(place == 0)
         def _():
@@ -409,16 +411,16 @@
             copy(stage, part).wait_send()
         for distance in range(hops):
 
-            @pl.when((place > 0) & in_window(distance))
+            @pl.when(reaches_below(distance))
             def _():
                 query_copy(distance, part).wait_send()
 
-            @pl.when(in_window(distance + 1))
+            @pl.when(place == far_place if distance == hops - 1 else in_window(distance + 1))
             def _():
                 parts_copy(distance + 1, part).wait_send()
 
 
-def mix(start, query, key, value, weight):
+def mix(far_place, start, query, key, value, weight):
     rows, width = query.shape
     devices, n = lax.axis_size("ctx"), lax.axis_size("head")
     hops = devices // 2
@@ -426,7 +428,7 @@
     stages = n.bit_length() - 1
     vmem = pl.BlockSpec(memory_space=pltpu.VMEM)
     return pl.pallas_call(
-        functools.partial(mix_kernel, devices, n, MIX_ROWS),
+        functools.partial(mix_kernel, devices, n, MIX_ROWS, far_place),
         out_shape=jax.ShapeDtypeStruct((rows, width), jnp.float32),
         in_specs=[vmem] * 4 + [pl.BlockSpec(memory_space=pl.ANY)],
         out_specs=vmem,
@@ -448,7 +450,7 @@
             pltpu.SemaphoreType.DMA((stages, chunks)),
         ],
         compiler_params=pltpu.CompilerParams(
-            collective_id=0, has_side_effects=True, vmem_limit_bytes=60 * 2**20
+            collective_id=far_place, has_side_effects=True, vmem_limit_bytes=60 * 2**20
         ),
         cost_estimate=pl.CostEstimate(flops=13 * 10**9, bytes_accessed=24 * 2**20, transcendentals=6 * 10**6),
     )(start, query, key, value, weight)
@@ -479,7 +481,10 @@
         earlier = jnp.sum((segment_ids[None, :] < segments[:, None]).astype(jnp.int32), axis=1)
         document_start.append(earlier - offset)
     start = jnp.stack(document_start)[..., None]
-    projected = mix(start, attn_query, attn_key, attn_value, out_weight)
+    reaches = segment_ids[num_rows - 1 : hops * num_rows : num_rows] == segment_ids[hops * num_rows :: num_rows]
+    far_place = jnp.sum(jnp.where(reaches, jnp.arange(hops, dtype=jnp.int32), 0))
+    variants = [functools.partial(mix, at) for at in range(hops)]
+    projected = lax.switch(far_place, variants, start, attn_query, attn_key, attn_value, out_weight)
     hyena_out, stream = hyena(rim, hyena_query, hyena_key, hyena_value, hyena_filter, projected)
     return (hyena_out, stream)
 

time: 137 us -> 130 us (0.949); the launches traced: 135 us -> 129 us
  Pallas kernels: 123 us -> 113 us
  local copies, waits for them, and re-layouts: 3.69 us -> 6.23 us
    pallas_call x1, Pallas kernels: 117 us -> 107 us  [mix(): pl.pallas_call(functools.partial(mix_kernel, devices, n, MIX_ROWS, far_pl...]
    slice x0 -> x2, local copies, waits for them, and re-layouts: none -> 1.55 us  [the longest x1 0.78 us: on_device(): segment_ids[num_rows - 1:hops * num_rows:num_rows]]
  transfers between devices with their start and end apart: 1 -> 1, of which waited for: 0 -> 0; matrix products, arithmetic and copies ran while one was open for 3% -> 5% of each run, Pallas kernels for 87% -> 83%
where the time goes in v3:
time: 130 us; the launch traced here: 129 us
  Pallas kernels  113 us (87%)
  local copies, waits for them, and re-layouts  6.23 us (5%)
  other arithmetic  4.67 us (4%)
  starting transfers between devices  3.47 us (3%)
  between operations  1.43 us (1%)
    pallas_call x1, Pallas kernels, mix(): pl.pallas_call(functools.partial(mix_kernel, devices, n, MIX_ROWS, far_pl...  107 us
    pallas_call x1, Pallas kernels, hyena(): pl.pallas_call(hyena_kernel, out_shape=[jax.ShapeDtypeStruct((rows, width...  6.28 us
    ppermute x1, starting transfers between devices, shifted(): return lax.ppermute(x, axis, pairs)  3.47 us
    unnamed x16, local copies, waits for them, and re-layouts  2.61 us
  transfers between devices with their start and end apart: 1, of which 0 were waited for; matrix products, arithmetic and copies ran while one was open for 5% of the time, Pallas kernels for 83%

profile of v3, /device:TPU:16, one launch (start us, length us, event | category | flops | bytes accessed | tf_op | source)
XLA Modules:
  0.0 129.2 jit_solution(8804139113527100012)
XLA Ops:
  0.6 1.8 %multiply_convert_fusion = bf16[128,1024]{1,0:T(8,128)(2,1)} fusion(bf16[512,1024]{1,0:T(8,128)(2,1)} %value_ref.1, bf16[512,1024]{1,0:T(8,128)(2,1)} %key_ref.1), kind=kLoop, calls=%fused_computation.3 | loop fusion | flops 524288 | bytes 786432 | tf_op jit(solution)/shard_map/convert_element_type | solution.py:475
  2.4 3.5 %collective-permute-start = (bf16[128,1024]{1,0:T(8,128)(2,1)}, bf16[128,1024]{1,0:T(8,128)(2,1)}, u32[]{:S(2)}, u32[]{:S(2)}) collective-permute-start(bf16[128,1024]{1,0:T(8,128)(2,1)} %multiply_convert_fusion), channel_id=1, source_target_pairs={{0,8},{8,16},{16,24},{1,9},{9,17},{17,25},{2,10},{10,18},{18,26},{... | collective-permute-start | bytes 786440 | tf_op jit(solution)/shard_map/ppermute | solution.py:21
  5.9 0.8 slice.14
  6.7 0.8 slice.15
  7.5 0.6 fusion
  8.8 0.9 fusion.1
  9.6 2.2 %convert_reduce_fusion.2 = (s32[512]{0:T(512)S(1)}, s32[512]{0:T(512)S(1)}, s32[512]{0:T(512)S(1)}) fusion(s32[2048]{0:T(1024)} %param.20, s32[512]{0:T(512)S(1)} %get-tuple-element.59, s32[512]{0:T(512)S(1)} %get-tuple-element.60, s32[512]{0:T(512)S(1)} %get-tuple-element.58), kind=kLoop, calls=%fused_computation.2 | loop fusion | flops 9435648 | bytes 20480 | tf_op jit(solution)/shard_map/reduce_sum | solution.py:481
  11.9 0.0 copy-start
  11.9 0.0 copy-start.1
  11.9 0.0 copy-start.2
  11.9 0.0 copy-start.3
  12.0 0.0 copy-start.4
  12.0 108.3 %conditional.1 = (f32[512,1024]{1,0:T(8,128)}) conditional(s32[]{:T(128)} %clamp.3, (s32[3,512,1]{1,0,2:T(4,128)S(1)}, bf16[512,1024]{1,0:T(8,128)(2,1)}, bf16[512,1024]{1,0:T(8,128)(2,1)}, bf16[512,1024]{1,0:T(8,128)(2,1)}, bf16[1024,8192]{1,0:T(8,128)(2,1)}) %tuple.13, (s32[3,512,1]{1,0,2:T(4,128)S(1)}, bf16[512,1024]{1,0:T(8,128)(2,1)}, ...), branch_computations={%region_4.5_spmd, %region_5.6_spmd} | conditional | flops 12999999488 | bytes 25178120 | solution.py:487
  12.0 1.2 copy.15.start_ref
  13.2 106.9 %branch_0_fun.1 = f32[512,1024]{1,0:T(8,128)} custom-call(s32[3,512,1]{2,1,0:T(8,128)} %copy.15.start_ref, bf16[512,1024]{1,0:T(8,128)(2,1)} %get-tuple-element.24.query_ref, bf16[512,1024]{1,0:T(8,128)(2,1)} %get-tuple-element.25.key_ref, bf16[512,1024]{1,0:T(8,128)(2,1)} %get-tuple-element.26.value_ref, bf16[1024,8192]{1,0:T(8,128)(2,1)} %get-tuple-element.27.weight_ref), custom_call_target="tpu_custom_call" | custom-call | flops 12999999488 | bytes 25165824 | tf_op jit(solution)/shard_map/cond/branch_0_fun/pallas_call | solution.py:430
  120.3 0.0 collective-permute-done.rim_ref
  120.3 0.0 copy-done
  120.3 0.0 copy-done.1
  120.3 0.0 copy-done.2
  120.3 0.0 copy-done.3
  120.4 0.0 copy-done.4
  120.4 0.0 copy-start.5
  120.4 0.9 copy-done.5
  121.3 0.0 copy-start.6
  121.3 0.8 copy-done.6
  122.1 0.0 copy-start.7
  122.1 0.8 copy-done.7
  123.0 6.3 %shard_map.122 = (bf16[512,1024]{1,0:T(8,128)(2,1)}, bf16[512,1024]{1,0:T(8,128)(2,1)}) custom-call(bf16[128,1024]{1,0:T(8,128)(2,1)} %collective-permute-done.rim_ref, bf16[512,1024]{1,0:T(8,128)(2,1)S(1)} %copy-done.2, bf16[512,1024]{1,0:T(8,128)(2,1)S(1)} %copy-done.1, bf16[512,1024]{1,0:T(8,128)(2,1)S(1)} %copy-done, bf16[128,1024]{1,0:T(8,128)(2,1)S(1)} %copy-done.3, ...), custom_call_target="tpu_custom_call" | custom-call | flops 3000000000 | bytes 5242880 | tf_op jit(solution)/shard_map/pallas_call | solution.py:84
  (3 shorter events, 0.0 us)
Async XLA Ops:
  2.4 117.9 %collective-permute-start = (bf16[128,1024]{1,0:T(8,128)(2,1)}, bf16[128,1024]{1,0:T(8,128)(2,1)}, u32[]{:S(2)}, u32[]{:S(2)}) collective-permute-start(bf16[128,1024]{1,0:T(8,128)(2,1)} %multiply_convert_fusion), channel_id=1, source_target_pairs={{0,8},{8,16},{16,24},{1,9},{9,17},{17,25},{2,10},{10,18},{18,26},{... | collective-permute-start | bytes 786440 | tf_op jit(solution)/shard_map/ppermute | solution.py:21
  11.9 108.4 %copy-start = (bf16[512,1024]{1,0:T(8,128)(2,1)S(1)}, bf16[512,1024]{1,0:T(8,128)(2,1)}, u32[]{:S(2)}) copy-start(bf16[512,1024]{1,0:T(8,128)(2,1)} %value_ref.1) | copy-start | bytes 3145732
  11.9 108.4 %copy-start.1 = (bf16[512,1024]{1,0:T(8,128)(2,1)S(1)}, bf16[512,1024]{1,0:T(8,128)(2,1)}, u32[]{:S(2)}) copy-start(bf16[512,1024]{1,0:T(8,128)(2,1)} %key_ref.1) | copy-start | bytes 3145732
  11.9 108.4 %copy-start.2 = (bf16[512,1024]{1,0:T(8,128)(2,1)S(1)}, bf16[512,1024]{1,0:T(8,128)(2,1)}, u32[]{:S(2)}) copy-start(bf16[512,1024]{1,0:T(8,128)(2,1)} %query_ref.1) | copy-start | bytes 3145732
  11.9 108.4 %copy-start.3 = (bf16[128,1024]{1,0:T(8,128)(2,1)S(1)}, bf16[128,1024]{1,0:T(8,128)(2,1)}, u32[]{:S(2)}) copy-start(bf16[128,1024]{1,0:T(8,128)(2,1)} %taps_ref.1) | copy-start | bytes 786436
  12.0 108.4 %copy-start.4 = (bf16[256,256]{1,0:T(8,128)(2,1)S(1)}, bf16[256,256]{1,0:T(8,128)(2,1)}, u32[]{:S(2)}) copy-start(bf16[256,256]{1,0:T(8,128)(2,1)} %constant.23.fh_ref) | copy-start | bytes 393220
  120.4 0.9 copy-start.5
  121.3 0.8 copy-start.6
  122.1 0.8 copy-start.7
